TPU v7x, 32 devices: a whole 2x2x4 slice. The times are simulated.
32 devices in a mesh: tm: 4 (over y, x), space: 8 (over z, core).
Axes of the slice: x: 2, y: 2, z: 4, core: 2. Of those that a mesh axis runs over, the one named last changes fastest.
Arguments:
- latent_clip: bfloat16 [8, 16, 32, 256], P('tm', 'space'), may hold values from -45 to 45
- cotangent: bfloat16 [8, 16, 32, 128], P('tm', 'space'), may hold values from -6 to 6
- conv_weight: bfloat16 [6912, 128], replicated, may hold values from -0.078125 to 0.078125
- norm_gain: float32 [256], replicated, may hold values from 0.5 to 1.5
- norm_shift: float32 [256], replicated, may hold values from -2 to 2
Outputs:
- clip_grad: bfloat16 [8, 16, 32, 256], P('tm', 'space')
- weight_grad: float32 [6912, 128], P('space')
- gain_grad: float32 [256], replicated
- shift_grad: float32 [256], replicated
All inputs are finite; a program needn't handle non-finite values.
Results may differ from a plain program's by a relative error of at most 0.0029.
Values may be sent and summed in bfloat16 or wider, within the bound.
A program may use at most 64 MiB of HBM per device.

v0:
```python
import jax
import jax.numpy as jnp
from jax import lax
from jax.sharding import PartitionSpec as P

GROUPS = 32


def shifted(value, axis, steps):
    count = lax.axis_size(axis)
    leading, last = (max(0, -steps), min(count, count - steps))
    return lax.ppermute(value, axis, [(source, source + steps) for source in range(leading, last)])


def extended_2(block, sides, width):
    for axis, dim in sides:
        count = lax.axis_size(axis)
        forward = [(i, i + 1) for i in range(count - 1)]
        backward = [(target, source) for source, target in forward]
        low = lax.ppermute(
            lax.slice_in_dim(block, block.shape[dim] - width, None, axis=dim), axis, forward
        )
        high = lax.ppermute(lax.slice_in_dim(block, 0, width, axis=dim), axis, backward)
        block = jnp.concatenate([low, block, high], axis=dim)
    return block


def silu_slope(activation):
    sigma = jax.nn.sigmoid(activation)
    return sigma * (1.0 + activation * (1.0 - sigma))


def tap_block(source, anchors, frame_count, row_count, col_count):
    pieces = [
        source[
            anchor[0] : anchor[0] + frame_count,
            anchor[1] : anchor[1] + row_count,
            anchor[2] : anchor[2] + col_count,
            :,
        ]
        for anchor in anchors
    ]
    merged = jnp.concatenate(pieces, axis=-1)
    return merged.reshape(frame_count * row_count * col_count, merged.shape[-1])


def transposed(grad_pad, conv_weight, frame_count, row_count, col_count):
    out_channels = conv_weight.shape[1]
    channels = conv_weight.shape[0] // 27
    kernel = conv_weight.reshape(3, 3, 3, channels, out_channels)
    total = jnp.zeros((frame_count * row_count * col_count, channels), jnp.float32)
    for tap_time in range(3):
        anchors = [
            (2 - tap_time, 2 - tap_row, 2 - tap_col) for tap_row in range(3) for tap_col in range(3)
        ]
        tap_cols = tap_block(grad_pad, anchors, frame_count, row_count, col_count)
        flipped = jnp.transpose(kernel[tap_time], (0, 1, 3, 2)).reshape(9 * out_channels, channels)
        total = total + jnp.dot(tap_cols, flipped, preferred_element_type=jnp.float32)
    return total.reshape(frame_count, row_count, col_count, channels)


def shards(latent_clip, cotangent, conv_weight, norm_gain, norm_shift):
    frame_count, row_count, col_count, channels = latent_clip.shape
    out_channels = cotangent.shape[-1]
    width_group = channels // GROUPS
    tm_size = lax.axis_size("tm")
    space_size = lax.axis_size("space")
    group_count = frame_count * row_count * col_count * width_group * tm_size * space_size
    values = latent_clip.astype(jnp.float32).reshape(
        frame_count, row_count, col_count, GROUPS, width_group
    )
    group_mean = lax.psum(jnp.sum(values, axis=(0, 1, 2, 4)), ("tm", "space")) / group_count
    centered = values - group_mean[:, None]
    group_var = (
        lax.psum(jnp.sum(centered * centered, axis=(0, 1, 2, 4)), ("tm", "space")) / group_count
    )
    inv_std = lax.rsqrt(group_var + 1e-06)
    normed = (centered * inv_std[:, None]).reshape(frame_count, row_count, col_count, channels)
    activation = normed * norm_gain + norm_shift
    hidden = jax.nn.silu(activation).astype(jnp.bfloat16)
    ahead = shifted(cotangent, "tm", -1)
    time_source = jnp.concatenate([cotangent, ahead], axis=0)
    time_pad = (0, 0)
    cached = shifted(hidden, "tm", 1)
    extended = jnp.concatenate([cached, hidden], axis=0)
    rimmed = extended_2(extended, (("space", 1),), 1)
    padded = jnp.pad(rimmed, ((0, 0), (0, 0), (1, 1), (0, 0)))
    cell_count = frame_count * row_count * col_count
    upstream = cotangent.reshape(cell_count, out_channels)
    tap_grads = []
    for tap_time in range(3):
        anchors = [(tap_time, tap_row, tap_col) for tap_row in range(3) for tap_col in range(3)]
        tap_cols = tap_block(padded, anchors, frame_count, row_count, col_count)
        tap_grads.append(
            lax.dot_general(
                tap_cols, upstream, (((0,), (0,)), ((), ())), preferred_element_type=jnp.float32
            )
        )
    local_grad = jnp.concatenate(tap_grads, axis=0)
    space_shard = lax.psum_scatter(local_grad, "space", scatter_dimension=0, tiled=True)
    weight_grad = lax.psum(space_shard, "tm")
    grad_pad = jnp.pad(time_source, (time_pad, (2, 2), (1, 1), (0, 0)))
    spread = transposed(grad_pad, conv_weight, frame_count, row_count + 2, col_count)
    from_below = shifted(spread[:, 0], "space", -1)
    from_above = shifted(spread[:, row_count + 1], "space", 1)
    inner = spread[:, 1 : row_count + 1]
    inner = inner.at[:, row_count - 1].add(from_below)
    inner = inner.at[:, 0].add(from_above)
    activation_grad = inner * silu_slope(activation)
    gain_grad, shift_grad = lax.psum(
        (
            jnp.sum(activation_grad * normed, axis=(0, 1, 2)),
            jnp.sum(activation_grad, axis=(0, 1, 2)),
        ),
        ("tm", "space"),
    )
    first = jnp.sum((norm_gain * shift_grad).reshape(GROUPS, width_group), axis=1)
    second = jnp.sum((norm_gain * gain_grad).reshape(GROUPS, width_group), axis=1)
    scaled = (activation_grad * norm_gain).reshape(
        frame_count, row_count, col_count, GROUPS, width_group
    )
    normed_groups = normed.reshape(frame_count, row_count, col_count, GROUPS, width_group)
    clip_grad = inv_std[:, None] * (
        scaled - first[:, None] / group_count - normed_groups * second[:, None] / group_count
    )
    clip_grad = clip_grad.reshape(frame_count, row_count, col_count, channels).astype(jnp.bfloat16)
    return (clip_grad, weight_grad, gain_grad, shift_grad)


def solution(mesh):
    return jax.shard_map(
        shards,
        mesh=mesh,
        in_specs=(P("tm", "space", None, None), P("tm", "space", None, None), P(), P(), P()),
        out_specs=(P("tm", "space", None, None), P("space", None), P(), P()),
        check_vma=False,
    )
```

profile of v0, /device:TPU:0, one launch (start us, length us, event | category | flops | bytes accessed | tf_op | source)
XLA Modules:
  0.0 225.5 jit_solution(13261450040164895884)
XLA Ops:
  7.2 0.9 convert_reduce_fusion
  8.1 0.1 reduce_sum.69
  8.2 0.1 reduce_sum.70
  8.3 1.3 collective-permute-start
  9.6 43.2 %psum.35 = f32[32]{0:T(128)S(1)} all-reduce(f32[32]{0:T(128)S(1)} %reduce_sum.70), channel_id=1, replica_groups=mesh['tm'=4,'space'=8] {'tm','space'}, use_global_device_ids=true, to_apply=%region_2.0 | all-reduce | flops 32 | bytes 256 | tf_op jit(solution)/shard_map/psum | solution.py:72
  52.8 0.1 sub.35
  52.8 0.1 sub.36
  52.9 0.9 fusion.33
  53.8 0.1 reduce_sum.72
  53.9 0.1 reduce_sum.73
  54.0 1.5 fusion.40
  55.6 41.0 %psum.36 = f32[32]{0:T(128)S(1)} all-reduce(f32[32]{0:T(128)S(1)} %reduce_sum.73), channel_id=1, replica_groups=mesh['tm'=4,'space'=8] {'tm','space'}, use_global_device_ids=true, to_apply=%region_5.6 | all-reduce | flops 32 | bytes 256 | tf_op jit(solution)/shard_map/psum | solution.py:75
  96.6 0.2 copy.15
  96.8 0.2 copy.13
  97.1 0.2 copy.14
  97.3 0.2 copy-done.1
  97.8 0.1 constant_dynamic-update-slice_fusion.23
  98.0 0.1 constant_dynamic-update-slice_fusion.20
  98.1 0.1 constant_dynamic-update-slice_fusion.19
  98.3 0.3 fusion.42
  98.6 0.3 convolution_add_fusion.1
  99.0 0.3 convolution_add_fusion
  99.4 1.3 collective-permute-start.1
  100.8 0.1 mul.76
  100.9 3.0 %collective-permute-start.2 = (f32[2,32,256]{2,1,0:T(8,128)S(1)}, f32[2,32,256]{2,1,0:T(8,128)S(1)}, u32[]{:S(2)}, u32[]{:S(2)}) collective-permute-start(f32[2,32,256]{2,1,0:T(8,128)S(1)} %get-tuple-element.53), channel_id=1, source_target_pairs={{0,1},{1,2},{2,3},{3,4},{4,5},{5,6},{6,7},{8,9},{9,10},{10,11},{11... | collective-permute-start | bytes 196616 | tf_op jit(solution)/shard_map/ppermute | solution.py:12
  103.9 0.9 collective-permute-done.2
  104.8 0.1 fusion.38
  105.0 4.2 %collective-permute-start.3 = (bf16[2,2,32,256]{3,2,1,0:T(8,128)(2,1)S(1)}, bf16[2,2,32,256]{3,2,1,0:T(8,128)(2,1)S(1)}, u32[]{:S(2)}, u32[]{:S(2)}) collective-permute-start(bf16[2,2,32,256]{3,2,1,0:T(8,128)(2,1)S(1)} %get-tuple-element.90), channel_id=1, source_target_pairs={{0,8},{8,16},{16,24},{1,9},{9,17},{17,25},{2,10},{10,18},{18,26},{... | collective-permute-start | bytes 196616 | tf_op jit(solution)/shard_map/ppermute | solution.py:12
  109.1 1.9 collective-permute-done.3
  111.1 1.4 collective-permute-start.4
  112.6 1.3 collective-permute-start.5
  113.9 4.6 %collective-permute-done.5 = bf16[4,1,32,256]{3,2,1,0:T(8,128)(2,1)S(1)} collective-permute-done((bf16[4,1,32,256]{3,2,1,0:T(8,128)(2,1)S(1)}, bf16[4,1,32,256]{3,2,1,0:T(8,128)(2,1)S(1)}, u32[]{:S(2)}, u32[]{:S(2)}) %collective-permute-start.5) | collective-permute-done | bytes 65568 | tf_op jit(solution)/shard_map/ppermute | solution.py:23
  118.4 0.1 select_maximum_fusion
  118.9 0.3 convolution_bitcast_fusion
  119.2 0.3 convolution_bitcast_fusion.2
  119.6 0.3 convolution_bitcast_fusion.1
  119.9 2.0 pad_maximum_fusion
  122.0 45.1 %all-reduce.2 = (f32[256]{0:T(256)S(1)}, f32[256]{0:T(256)S(1)}) all-reduce(f32[256]{0:T(256)S(1)} %get-tuple-element.29, f32[256]{0:T(256)S(1)} %get-tuple-element.28), channel_id=1, replica_groups=mesh['tm'=4,'space'=8] {'tm','space'}, use_global_device_ids=true, to_apply=%region_10.11 | all-reduce | flops 512 | bytes 4096 | tf_op jit(solution)/shard_map/psum | solution.py:110
  167.2 0.1 reshape.151
  167.2 0.1 reduce_sum.75
  167.4 3.1 %reduce-scatter.2.cloned.1.call-done = f32[864,128]{1,0:T(8,128)} async-done(((f32[6912,128]{1,0:T(8,128)}), f32[864,128]{1,0:T(8,128)}) %reduce-scatter.2.cloned.1.call-update) | async-done | bytes 442384 | tf_op jit(solution)/shard_map/reduce_scatter | solution.py:100
  170.6 0.1 sub.41
  170.7 0.1 reshape.152
  170.8 0.1 reduce_sum.77
  171.0 0.1 mul.89
  171.1 0.7 fusion.32
  171.8 45.1 %all-reduce.5.cloned.1.call-done = f32[864,128]{1,0:T(8,128)} async-done(((f32[864,128]{1,0:T(8,128)}), f32[864,128]{1,0:T(8,128)}) %all-reduce.5.cloned.1.call-update) | async-done | bytes 442384 | tf_op jit(solution)/shard_map/psum | solution.py:101
  216.9 1.8 copy.74
  (51 shorter events, 1.1 us)
Async XLA Ops:
  7.2 163.3 %reduce-scatter.2.cloned.1.call-start = ((), (), s32[]{:S(2)}) async-start(), calls=%async_computation.1 | async-start | bytes 3981312 | tf_op jit(solution)/shard_map/reduce_scatter | solution.py:100
  8.3 89.0 %collective-permute-start = (bf16[2,2,32,128]{3,2,1,0:T(8,128)(2,1)}, bf16[2,2,32,128]{3,2,1,0:T(8,128)(2,1)S(1)}, u32[]{:S(2)}, u32[]{:S(2)}) collective-permute-start(bf16[2,2,32,128]{3,2,1,0:T(8,128)(2,1)} %param.10), channel_id=1, source_target_pairs={{8,0},{16,8},{24,16},{9,1},{17,9},{25,17},{10,2},{18,10},{26,18},{... | collective-permute-start | bytes 98312 | tf_op jit(solution)/shard_map/ppermute | solution.py:12
  96.8 0.8 copy-start.1
  99.0 5.8 %copy-start = (bf16[2,2,32,256]{3,2,1,0:T(8,128)(2,1)S(1)}, bf16[2,2,32,256]{3,2,1,0:T(8,128)(2,1)}, u32[]{:S(2)}) copy-start(bf16[2,2,32,256]{3,2,1,0:T(8,128)(2,1)} %param.9) | copy-start | bytes 196612
  99.0 5.8 %copy-start.2 = (f32[256]{0:T(256)S(1)}, f32[256]{0:T(256)}, u32[]{:S(2)}) copy-start(f32[256]{0:T(256)} %param.12) | copy-start | bytes 3076
  99.0 5.8 %copy-start.3 = (f32[256]{0:T(256)S(1)}, f32[256]{0:T(256)}, u32[]{:S(2)}) copy-start(f32[256]{0:T(256)} %param.13) | copy-start | bytes 3076
  99.4 4.5 %collective-permute-start.1 = (f32[2,32,256]{2,1,0:T(8,128)S(1)}, f32[2,32,256]{2,1,0:T(8,128)S(1)}, u32[]{:S(2)}, u32[]{:S(2)}) collective-permute-start(f32[2,32,256]{2,1,0:T(8,128)S(1)} %get-tuple-element.54), channel_id=1, source_target_pairs={{1,0},{2,1},{3,2},{4,3},{5,4},{6,5},{7,6},{9,8},{10,9},{11,10},{12... | collective-permute-start | bytes 196616 | tf_op jit(solution)/shard_map/ppermute | solution.py:12
  100.9 3.9 %collective-permute-start.2 = (f32[2,32,256]{2,1,0:T(8,128)S(1)}, f32[2,32,256]{2,1,0:T(8,128)S(1)}, u32[]{:S(2)}, u32[]{:S(2)}) collective-permute-start(f32[2,32,256]{2,1,0:T(8,128)S(1)} %get-tuple-element.53), channel_id=1, source_target_pairs={{0,1},{1,2},{2,3},{3,4},{4,5},{5,6},{6,7},{8,9},{9,10},{10,11},{11... | collective-permute-start | bytes 196616 | tf_op jit(solution)/shard_map/ppermute | solution.py:12
  105.0 6.1 %collective-permute-start.3 = (bf16[2,2,32,256]{3,2,1,0:T(8,128)(2,1)S(1)}, bf16[2,2,32,256]{3,2,1,0:T(8,128)(2,1)S(1)}, u32[]{:S(2)}, u32[]{:S(2)}) collective-permute-start(bf16[2,2,32,256]{3,2,1,0:T(8,128)(2,1)S(1)} %get-tuple-element.90), channel_id=1, source_target_pairs={{0,8},{8,16},{16,24},{1,9},{9,17},{17,25},{2,10},{10,18},{18,26},{... | collective-permute-start | bytes 196616 | tf_op jit(solution)/shard_map/ppermute | solution.py:12
  111.1 2.8 %collective-permute-start.4 = (bf16[4,1,32,256]{3,2,1,0:T(8,128)(2,1)S(1)}, bf16[4,1,32,256]{3,2,1,0:T(8,128)(2,1)S(1)}, u32[]{:S(2)}, u32[]{:S(2)}) collective-permute-start(bf16[4,1,32,256]{3,2,1,0:T(8,128)(2,1)S(1)} %get-tuple-element.88), channel_id=1, source_target_pairs={{0,1},{1,2},{2,3},{3,4},{4,5},{5,6},{6,7},{8,9},{9,10},{10,11},{11... | collective-permute-start | bytes 196616 | tf_op jit(solution)/shard_map/ppermute | solution.py:20
  112.6 5.9 %collective-permute-start.5 = (bf16[4,1,32,256]{3,2,1,0:T(8,128)(2,1)S(1)}, bf16[4,1,32,256]{3,2,1,0:T(8,128)(2,1)S(1)}, u32[]{:S(2)}, u32[]{:S(2)}) collective-permute-start(bf16[4,1,32,256]{3,2,1,0:T(8,128)(2,1)S(1)} %get-tuple-element.89), channel_id=1, source_target_pairs={{1,0},{2,1},{3,2},{4,3},{5,4},{6,5},{7,6},{9,8},{10,9},{11,10},{12... | collective-permute-start | bytes 196616 | tf_op jit(solution)/shard_map/ppermute | solution.py:23
  122.0 94.9 %all-reduce.5.cloned.1.call-start = ((), (), s32[]{:S(2)}) async-start(), calls=%async_computation.2 | async-start | bytes 884736 | tf_op jit(solution)/shard_map/psum | solution.py:101
  167.2 51.5 %copy-start.4 = (f32[256]{0:T(256)}, f32[256]{0:T(256)S(1)}, u32[]{:S(2)}) copy-start(f32[256]{0:T(256)S(1)} %get-tuple-element.97) | copy-start | bytes 3076
  167.2 51.5 %copy-start.5 = (f32[256]{0:T(256)}, f32[256]{0:T(256)S(1)}, u32[]{:S(2)}) copy-start(f32[256]{0:T(256)S(1)} %get-tuple-element.98) | copy-start | bytes 3076
Sparse Core Ops, SparseCore 0:
  122.1 48.3 reduce-scatter.1
  173.8 43.0 all-reduce.4
where the time goes:
time: 226 us
  blocking collectives  129 us (57%)
  waiting for transfers between devices  55.6 us (25%)
  between operations  14.5 us (6%)
  starting transfers between devices  12.6 us (6%)
  local copies, waits for them, and re-layouts  6.15 us (3%)
  other arithmetic  5.25 us (2%)
    psum x1, blocking collectives, shards(): lax.psum((jnp.sum(activation_grad * normed, axis=(0, 1, 2)), jnp.sum(acti...  45.1 us
    psum x1, waiting for transfers between devices, shards(): weight_grad = lax.psum(space_shard, 'tm')  45.1 us
    psum x1, blocking collectives, shards(): lax.psum(jnp.sum(values, axis=(0, 1, 2, 4)), ('tm', 'space')) / group_count  43.2 us
    psum x1, blocking collectives, shards(): lax.psum(jnp.sum(centered * centered, axis=(0, 1, 2, 4)), ('tm', 'space'))  41 us
    ppermute x4, starting transfers between devices, shifted(): lax.ppermute(value, axis, [(source, source + steps) for source in range(l...  9.8 us
    ppermute x1, waiting for transfers between devices, extended_2(): lax.ppermute(lax.slice_in_dim(block, 0, width, axis=dim), axis, backward)  4.55 us
  transfers between devices with their start and end apart: 8, of which 5 were waited for; matrix products, arithmetic and copies ran while one was open for 2% of the time, Pallas kernels for 0%

commit v1 on v0

--- a/solution.py
+++ b/solution.py
@@ -1,9 +1,283 @@
+import functools
+
 import jax
 import jax.numpy as jnp
 from jax import lax
+from jax.experimental import pallas as pl
+from jax.experimental.pallas import tpu as pltpu
 from jax.sharding import PartitionSpec as P
 
 GROUPS = 32
+UNIT = 32
+
+
+def fused_kernel(
+    T, S, shard, chunk,
+    x_ref, c_ref, w_hbm, gain_ref, shift_ref,
+    clip_ref, wg_out, gg_ref, sg_ref,
+    w_ref, xg, cg, g3, st1, st2, gr1, gr2, hg, ht, wg, pbuf, sbuf, rbuf, abuf,
+    send_sem, recv_sem, w_sem,
+):
+    F, R, W, C = x_ref.shape
+    O = c_ref.shape[-1]
+    Z = S // 2
+    cells = F * R * W
+    j = lax.axis_index("tm")
+    s = lax.axis_index("space")
+    z = s // 2
+    core = s % 2
+    wrap_s = lambda v: lax.rem(v + S, S)
+    wrap_j = lambda v: lax.rem(v + T, T)
+
+    w_copy = pltpu.make_async_copy(w_hbm, w_ref, w_sem)
+    w_copy.start()
+
+    peers = []
+    for dj in range(T):
+        for ds in range(S):
+            if (dj, ds) != (0, 0) and (dj == 0 or ds in (0, 1, S - 1)):
+                peers.append((wrap_j(j + dj), wrap_s(s + ds)))
+    barrier = pltpu.get_barrier_semaphore()
+    for peer in peers:
+        pl.semaphore_signal(barrier, inc=1, device_id=peer, device_id_type=pl.DeviceIdType.MESH)
+
+    counter = [0]
+
+    def remote(src, dst, peer):
+        k = counter[0]
+        counter[0] += 1
+        copy = pltpu.make_async_remote_copy(
+            src_ref=src, dst_ref=dst, send_sem=send_sem.at[k], recv_sem=recv_sem.at[k],
+            device_id=peer, device_id_type=pl.DeviceIdType.MESH,
+        )
+        copy.start()
+        return copy
+
+    x_own = x_ref[...].reshape(cells, C).astype(jnp.float32)
+    mean_own = jnp.sum(x_own, axis=0, keepdims=True) * (1.0 / cells)
+    centered_own = x_own - mean_own
+    m2_own = jnp.sum(centered_own * centered_own, axis=0, keepdims=True)
+    st1[s] = jnp.concatenate([mean_own, m2_own], axis=0)
+    xg[j] = x_ref[...]
+    cg[pl.ds(F * j, F), pl.ds(1, R)] = c_ref[...]
+
+    pl.semaphore_wait(barrier, len(peers))
+
+    started = []
+    s1 = [remote(st1.at[s], st1.at[s], (j, wrap_s(s + d))) for d in range(1, S)]
+    cots = []
+    for d in range(1, T):
+        cots.append(remote(c_ref, cg.at[pl.ds(F * j, F), pl.ds(1, R)], (wrap_j(j + d), s)))
+    for d in range(T):
+        cots.append(remote(
+            c_ref.at[:, pl.ds(R - 1, 1)], cg.at[pl.ds(F * j, F), pl.ds(0, 1)],
+            (wrap_j(j + d), wrap_s(s + 1))))
+        cots.append(remote(
+            c_ref.at[:, pl.ds(0, 1)], cg.at[pl.ds(F * j, F), pl.ds(R + 1, 1)],
+            (wrap_j(j + d), wrap_s(s - 1))))
+    xs = [remote(x_ref, xg.at[j], (wrap_j(j + d), s)) for d in range(1, T)]
+    started += s1 + cots + xs
+
+    def merge(slots, n, count):
+        mean = slots[0][0:1]
+        for k in range(1, n):
+            mean = mean + slots[k][0:1]
+        mean = mean * (1.0 / n)
+        m2 = jnp.zeros_like(mean)
+        for k in range(n):
+            delta = slots[k][0:1] - mean
+            m2 = m2 + slots[k][1:2] + count * (delta * delta)
+        return mean, m2
+
+    for copy in s1:
+        copy.wait_recv()
+    mean1, m21 = merge(st1, S, float(cells))
+    st2[j] = jnp.concatenate([mean1, m21], axis=0)
+    s2 = [remote(st2.at[j], st2.at[j], (wrap_j(j + d), s)) for d in range(1, T)]
+    started += s2
+
+    for copy in cots:
+        copy.wait_recv()
+    TF = T * F
+    n = TF * (R + 2) * W
+    val = cg[...].reshape(n, O).astype(jnp.float32)
+    idx = lax.broadcasted_iota(jnp.int32, (n, O), 0)
+    col = idx % W
+    row = (idx // W) % (R + 2)
+    off = ((row == 0) & (s == 0)) | ((row == R + 1) & (s == S - 1))
+    val = jnp.where(off, 0.0, val)
+    right = jnp.where(col == W - 1, 0.0, pltpu.roll(val, n - 1, 0))
+    left = jnp.where(col == 0, 0.0, pltpu.roll(val, 1, 0))
+    for c, piece in enumerate((right, val, left)):
+        g3[pl.ds(0, TF), :, :, c * O:(c + 1) * O] = piece.astype(jnp.bfloat16).reshape(TF, R + 2, W, O)
+    g3[pl.ds(TF, 2)] = jnp.zeros((2, R + 2, W, 3 * O), jnp.bfloat16)
+
+    w_copy.wait()
+    total = jnp.zeros((cells, C), jnp.float32)
+    for a in range(3):
+        for b in range(3):
+            block = g3[pl.ds(F * j + 2 - a, F), pl.ds(2 - b, R)].reshape(cells, 3 * O)
+            for c in range(3):
+                tap = (a * 3 + b) * 3 + c
+                total = total + lax.dot_general(
+                    block[:, c * O:(c + 1) * O], w_ref[tap * C:(tap + 1) * C],
+                    (((1,), (1,)), ((), ())), preferred_element_type=jnp.float32)
+    hg[...] = total
+
+    same = (
+        lax.broadcasted_iota(jnp.int32, (C, C), 0) // (C // GROUPS)
+        == lax.broadcasted_iota(jnp.int32, (C, C), 1) // (C // GROUPS)
+    ).astype(jnp.float32)
+
+    def group_sum(v):
+        wide = jnp.broadcast_to(v, (8, C))
+        return jnp.dot(wide, same, precision=lax.Precision.HIGHEST,
+                       preferred_element_type=jnp.float32)[0:1]
+
+    width = C // GROUPS
+    channel_count = float(cells * S * T)
+    count = channel_count * width
+    for copy in s2:
+        copy.wait_recv()
+    mean2, m22 = merge(st2, T, float(cells * S))
+    mean = group_sum(mean2) * (1.0 / width)
+    delta = mean2 - mean
+    var = group_sum(m22 + channel_count * (delta * delta)) * (1.0 / count)
+    inv = lax.rsqrt(var + 1e-06)
+    gain = gain_ref[...]
+    shift = shift_ref[...]
+
+    for copy in xs:
+        copy.wait_recv()
+    for k in range(T):
+        xk = xg[k].reshape(cells, C).astype(jnp.float32)
+        act = (xk - mean) * inv * gain + shift
+        hidden = act * jax.nn.sigmoid(act)
+        ht[:, k * cells:(k + 1) * cells] = jnp.transpose(hidden).astype(jnp.bfloat16)
+
+    start = jnp.minimum(chunk * j, shard - chunk)
+    rows = lambda target: pl.ds(pl.multiple_of(target * shard + start, 32), chunk)
+    hidden_t = ht[...]
+    pair = []
+    for a in range(3):
+        for b in range(3):
+            g = a * 3 + b
+            block = g3[pl.ds(2 - a, TF), pl.ds(2 - b, R)].reshape(T * cells, 3 * O)
+            out = jnp.dot(hidden_t, block, preferred_element_type=jnp.float32)
+            for c in range(3):
+                tap = g * 3 + c
+                wg[tap * C:(tap + 1) * C] = out[:, c * O:(c + 1) * O]
+            while len(pair) < Z and shard * 2 * (len(pair) + 1) <= 3 * C * (g + 1):
+                k = len(pair)
+                pair.append(remote(
+                    wg.at[rows(2 * k + 1 - core)], pbuf.at[k], (j, 2 * z + 1 - core)))
+    started += pair
+
+    normed = (x_own - mean) * inv
+    act = normed * gain + shift
+    sigma = jax.nn.sigmoid(act)
+    act_grad = hg[...] * (sigma * (1.0 + act * (1.0 - sigma)))
+    gr1[s] = jnp.concatenate(
+        [jnp.sum(act_grad * normed, axis=0, keepdims=True),
+         jnp.sum(act_grad, axis=0, keepdims=True)], axis=0)
+    g1 = [remote(gr1.at[s], gr1.at[s], (j, wrap_s(s + d))) for d in range(1, S)]
+    started += g1
+    hg[...] = act_grad
+
+    for copy in pair:
+        copy.wait_recv()
+    zs = []
+    for d in range(1, Z):
+        k = lax.rem(z + d, Z)
+        sbuf[d - 1] = (wg[rows(2 * k + core)] + pbuf[k]).astype(sbuf.dtype)
+        zs.append(remote(sbuf.at[d - 1], rbuf.at[d - 1], (j, 2 * k + core)))
+    started += zs
+
+    for copy in g1:
+        copy.wait_recv()
+    part = gr1[0]
+    for k in range(1, S):
+        part = part + gr1[k]
+    gr2[j] = part
+    g2 = [remote(gr2.at[j], gr2.at[j], (wrap_j(j + d), s)) for d in range(1, T)]
+    started += g2
+
+    acc = wg[rows(s)] + pbuf[z]
+    for d in range(1, Z):
+        zs[d - 1].wait_recv()
+        acc = acc + rbuf[d - 1].astype(jnp.float32)
+    abuf[j] = acc.astype(abuf.dtype)
+    ag = [remote(abuf.at[j], abuf.at[j], (wrap_j(j + d), s)) for d in range(1, T)]
+    started += ag
+
+    for copy in g2:
+        copy.wait_recv()
+    sums = gr2[0]
+    for k in range(1, T):
+        sums = sums + gr2[k]
+    gain_grad = sums[0:1]
+    shift_grad = sums[1:2]
+    gg_ref[...] = gain_grad
+    sg_ref[...] = shift_grad
+    first = group_sum(gain * shift_grad)
+    second = group_sum(gain * gain_grad)
+    normed = (x_own - mean) * inv
+    clip = inv * (hg[...] * gain - first * (1.0 / count) - normed * (second * (1.0 / count)))
+    clip_ref[...] = clip.astype(clip_ref.dtype).reshape(clip_ref.shape)
+
+    for copy in ag:
+        copy.wait_recv()
+    for k in range(T):
+        at = min(chunk * k, shard - chunk)
+        wg_out[at:at + chunk] = abuf[k].astype(jnp.float32)
+    for copy in started:
+        copy.wait_send()
+
+
+def fused_shards(T, S, latent_clip, cotangent, conv_weight, norm_gain, norm_shift):
+    F, R, W, C = latent_clip.shape
+    O = cotangent.shape[-1]
+    shard = conv_weight.shape[0] // S
+    chunk = -(-shard // (T * UNIT)) * UNIT
+    cells = F * R * W
+    Z = S // 2
+    copies = 2 * ((S - 1) + (T - 1)) + 2 * (T - 1) + 2 * T + Z + (Z - 1) + (T - 1)
+    vmem = pl.BlockSpec(memory_space=pltpu.VMEM)
+    f32, bf16 = jnp.float32, jnp.bfloat16
+    clip, wgrad, gg, sg = pl.pallas_call(
+        functools.partial(fused_kernel, T, S, shard, chunk),
+        out_shape=(
+            jax.ShapeDtypeStruct(latent_clip.shape, bf16),
+            jax.ShapeDtypeStruct((shard, O), f32),
+            jax.ShapeDtypeStruct((1, C), f32),
+            jax.ShapeDtypeStruct((1, C), f32),
+        ),
+        in_specs=[vmem, vmem, pl.BlockSpec(memory_space=pl.ANY), vmem, vmem],
+        out_specs=(vmem, vmem, vmem, vmem),
+        scratch_shapes=[
+            pltpu.VMEM(conv_weight.shape, bf16),
+            pltpu.VMEM((T, F, R, W, C), bf16),
+            pltpu.VMEM((T * F, R + 2, W, O), bf16),
+            pltpu.VMEM((T * F + 2, R + 2, W, 3 * O), bf16),
+            pltpu.VMEM((S, 2, C), f32),
+            pltpu.VMEM((T, 2, C), f32),
+            pltpu.VMEM((S, 2, C), f32),
+            pltpu.VMEM((T, 2, C), f32),
+            pltpu.VMEM((cells, C), f32),
+            pltpu.VMEM((C, T * cells), bf16),
+            pltpu.VMEM(conv_weight.shape, f32),
+            pltpu.VMEM((Z, chunk, O), f32),
+            pltpu.VMEM((Z - 1, chunk, O), bf16),
+            pltpu.VMEM((Z - 1, chunk, O), bf16),
+            pltpu.VMEM((T, chunk, O), bf16),
+            pltpu.SemaphoreType.DMA((copies,)),
+            pltpu.SemaphoreType.DMA((copies,)),
+            pltpu.SemaphoreType.DMA,
+        ],
+        compiler_params=pltpu.CompilerParams(
+            collective_id=0, has_side_effects=True, vmem_limit_bytes=40 * 1024 * 1024),
+    )(latent_clip, cotangent, conv_weight, norm_gain.reshape(1, C), norm_shift.reshape(1, C))
+    return clip, wgrad, gg.reshape(C), sg.reshape(C)
 
 
 def shifted(value, axis, steps):
@@ -128,8 +402,19 @@
 
 
 def solution(mesh):
+    T, S = mesh.shape["tm"], mesh.shape["space"]
+
+    def block(latent_clip, cotangent, conv_weight, norm_gain, norm_shift):
+        rows = conv_weight.shape[0] // S
+        aligned = rows % UNIT == 0 and rows >= T * UNIT and S % 2 == 0 and S > 2
+        if aligned:
+            body = functools.partial(fused_shards, T, S)
+        else:
+            body = shards
+        return body(latent_clip, cotangent, conv_weight, norm_gain, norm_shift)
+
     return jax.shard_map(
-        shards,
+        block,
         mesh=mesh,
         in_specs=(P("tm", "space", None, None), P("tm", "space", None, None), P(), P(), P()),
         out_specs=(P("tm", "space", None, None), P("space", None), P(), P()),

time: 226 us -> 36.9 us (0.16)
  blocking collectives: 129 us -> 0 us
  waiting for transfers between devices: 55.6 us -> 0 us
  Pallas kernels: 0 us -> 29 us
  between operations: 14.5 us -> 0.65 us
  starting transfers between devices: 12.6 us -> 0 us
  other arithmetic: 5.25 us -> 0 us
    psum x3 -> x0, blocking collectives: 129 us -> none  [the longest x1 45.1 us: shards(): lax.psum((jnp.sum(activation_grad * normed, axis=(0, 1, 2)), jnp.sum(acti...]
    psum x1 -> x0, waiting for transfers between devices: 45.1 us -> none  [shards(): weight_grad = lax.psum(space_shard, 'tm')]
    pallas_call x0 -> x1, Pallas kernels: none -> 29 us  [fused_shards(): pl.pallas_call(functools.partial(fused_kernel, T, S, shard, chunk), out_s...]
    ppermute x6 -> x0, starting transfers between devices: 12.5 us -> none  [the longest x4 9.8 us: shifted(): lax.ppermute(value, axis, [(source, source + steps) for source in range(l...]
    ppermute x6 -> x0, waiting for transfers between devices: 7.35 us -> none  [the longest x1 4.55 us: extended_2(): lax.ppermute(lax.slice_in_dim(block, 0, width, axis=dim), axis, backward)]
    unnamed x31 -> x14, local copies, waits for them, and re-layouts: 2.76 us -> 6.94 us
    reduce_scatter x1 -> x0, waiting for transfers between devices: 3.13 us -> none  [shards(): lax.psum_scatter(local_grad, 'space', scatter_dimension=0, tiled=True)]
    reduce_sum x7 -> x0, other arithmetic: 2.33 us -> none  [the longest x2 1 us: shards(): jnp.sum(centered * centered, axis=(0, 1, 2, 4))]
  transfers between devices with their start and end apart: 8 -> 0, of which waited for: 5 -> 0; matrix products, arithmetic and copies ran while one was open for 2% -> 0% of each run, Pallas kernels for 0% -> 0%
where the time goes in v1:
time: 36.9 us; the launch traced here: 36.6 us
  Pallas kernels  29 us (79%)
  local copies, waits for them, and re-layouts  6.94 us (19%)
  between operations  0.65 us (2%)
    pallas_call x1, Pallas kernels, fused_shards(): pl.pallas_call(functools.partial(fused_kernel, T, S, shard, chunk), out_s...  29 us
    unnamed x14, local copies, waits for them, and re-layouts  6.94 us

profile of v1, /device:TPU:0, one launch (start us, length us, event | category | flops | bytes accessed | tf_op | source)
XLA Modules:
  0.0 36.6 jit_solution(7840015554222920752)
XLA Ops:
  0.6 0.0 copy-start
  0.6 1.5 %copy-done = bf16[6912,128]{1,0:T(8,128)(2,1)S(1)} copy-done((bf16[6912,128]{1,0:T(8,128)(2,1)S(1)}, bf16[6912,128]{1,0:T(8,128)(2,1)}, u32[]{:S(2)}) %copy-start) | copy-done | bytes 1769496
  2.1 0.0 copy-start.1
  2.1 0.8 %copy-done.1 = bf16[2,2,32,256]{3,2,1,0:T(8,128)(2,1)S(1)} copy-done((bf16[2,2,32,256]{3,2,1,0:T(8,128)(2,1)S(1)}, bf16[2,2,32,256]{3,2,1,0:T(8,128)(2,1)}, u32[]{:S(2)}) %copy-start.1) | copy-done | bytes 65560
  2.9 0.0 copy-start.2
  3.0 0.8 %copy-done.2 = bf16[2,2,32,128]{3,2,1,0:T(8,128)(2,1)S(1)} copy-done((bf16[2,2,32,128]{3,2,1,0:T(8,128)(2,1)S(1)}, bf16[2,2,32,128]{3,2,1,0:T(8,128)(2,1)}, u32[]{:S(2)}) %copy-start.2) | copy-done | bytes 32792
  3.7 0.0 copy-start.3
  3.7 0.7 %copy-done.3 = f32[256]{0:T(256)S(1)} copy-done((f32[256]{0:T(256)S(1)}, f32[256]{0:T(256)}, u32[]{:S(2)}) %copy-start.3) | copy-done | bytes 1048
  4.4 0.0 copy-start.4
  4.4 0.7 %copy-done.4 = f32[256]{0:T(256)S(1)} copy-done((f32[256]{0:T(256)S(1)}, f32[256]{0:T(256)}, u32[]{:S(2)}) %copy-start.4) | copy-done | bytes 1048
  5.1 29.0 %shard_map.84 = (bf16[2,2,32,256]{3,2,1,0:T(8,128)(2,1)S(1)}, f32[864,128]{1,0:T(8,128)S(1)}, f32[1,256]{1,0:T(1,128)S(1)}, f32[1,256]{1,0:T(1,128)S(1)}) custom-call(bf16[2,2,32,256]{3,2,1,0:T(8,128)(2,1)S(1)} %copy-done.1, bf16[2,2,32,128]{3,2,1,0:T(8,128)(2,1)S(1)} %copy-done.2, bf16[6912,128]{1,0:T(8,128)(2,1)S(1)} %copy-done, f32[1,256]{1,0:T(1,128)S(1)} %bitcast.4, ...), custom_call_target="tpu_custom_call" | custom-call | tf_op jit(solution)/shard_map/pallas_call | solution.py:247
  34.1 0.6 %copy.13 = bf16[2,2,32,256]{3,2,1,0:T(8,128)(2,1)} copy(bf16[2,2,32,256]{3,2,1,0:T(8,128)(2,1)S(1)} %get-tuple-element.16) | data formatting | bytes 131072
  34.7 0.8 %copy.14 = f32[864,128]{1,0:T(8,128)} copy(f32[864,128]{1,0:T(8,128)S(1)} %get-tuple-element.17) | data formatting | bytes 884736
  35.5 0.6 %copy.15 = f32[256]{0:T(256)} copy(f32[256]{0:T(256)S(1)} %bitcast.7) | data formatting | bytes 2048
  36.0 0.6 %copy.16 = f32[256]{0:T(256)} copy(f32[256]{0:T(256)S(1)} %bitcast.6) | data formatting | bytes 2048
Async XLA Ops:
  0.6 1.5 %copy-start = (bf16[6912,128]{1,0:T(8,128)(2,1)S(1)}, bf16[6912,128]{1,0:T(8,128)(2,1)}, u32[]{:S(2)}) copy-start(bf16[6912,128]{1,0:T(8,128)(2,1)} %w_hbm.1) | copy-start | bytes 5308420
  2.1 0.8 %copy-start.1 = (bf16[2,2,32,256]{3,2,1,0:T(8,128)(2,1)S(1)}, bf16[2,2,32,256]{3,2,1,0:T(8,128)(2,1)}, u32[]{:S(2)}) copy-start(bf16[2,2,32,256]{3,2,1,0:T(8,128)(2,1)} %x_ref.1) | copy-start | bytes 196612
  2.9 0.8 %copy-start.2 = (bf16[2,2,32,128]{3,2,1,0:T(8,128)(2,1)S(1)}, bf16[2,2,32,128]{3,2,1,0:T(8,128)(2,1)}, u32[]{:S(2)}) copy-start(bf16[2,2,32,128]{3,2,1,0:T(8,128)(2,1)} %c_ref.1) | copy-start | bytes 98308
  3.7 0.7 %copy-start.3 = (f32[256]{0:T(256)S(1)}, f32[256]{0:T(256)}, u32[]{:S(2)}) copy-start(f32[256]{0:T(256)} %param.8) | copy-start | bytes 3076
  4.4 0.7 %copy-start.4 = (f32[256]{0:T(256)S(1)}, f32[256]{0:T(256)}, u32[]{:S(2)}) copy-start(f32[256]{0:T(256)} %param.9) | copy-start | bytes 3076

commit v2 on v1

--- a/solution.py
+++ b/solution.py
@@ -13,13 +13,13 @@
 
 def fused_kernel(
     T, S, shard, chunk,
-    x_ref, c_ref, w_hbm, gain_ref, shift_ref,
+    x_hbm, c_hbm, w_hbm, gain_hbm, shift_hbm,
     clip_ref, wg_out, gg_ref, sg_ref,
-    w_ref, xg, cg, g3, st1, st2, gr1, gr2, hg, ht, wg, pbuf, sbuf, rbuf, abuf,
-    send_sem, recv_sem, w_sem,
+    gain_ref, shift_ref, w_ref, xg, cg, g3, st1, st2, gr1, gr2, hg, ht, wg, pbuf, sbuf, rbuf, abuf,
+    send_sem, recv_sem, zs_sem, zr_sem, load_sem,
 ):
-    F, R, W, C = x_ref.shape
-    O = c_ref.shape[-1]
+    F, R, W, C = x_hbm.shape
+    O = c_hbm.shape[-1]
     Z = S // 2
     cells = F * R * W
     j = lax.axis_index("tm")
@@ -29,9 +29,6 @@
     wrap_s = lambda v: lax.rem(v + S, S)
     wrap_j = lambda v: lax.rem(v + T, T)
 
-    w_copy = pltpu.make_async_copy(w_hbm, w_ref, w_sem)
-    w_copy.start()
-
     peers = []
     for dj in range(T):
         for ds in range(S):
@@ -41,7 +38,19 @@
     for peer in peers:
         pl.semaphore_signal(barrier, inc=1, device_id=peer, device_id_type=pl.DeviceIdType.MESH)
 
+    x_own_ref = xg.at[j]
+    c_own_ref = cg.at[pl.ds(F * j, F), pl.ds(1, R)]
+    loads = [
+        pltpu.make_async_copy(source, target, load_sem.at[k])
+        for k, (source, target) in enumerate((
+            (x_hbm, x_own_ref), (c_hbm, c_own_ref), (gain_hbm, gain_ref),
+            (shift_hbm, shift_ref), (w_hbm, w_ref)))
+    ]
+    for load in loads:
+        load.start()
+
     counter = [0]
+    started = []
 
     def remote(src, dst, peer):
         k = counter[0]
@@ -51,32 +60,32 @@
             device_id=peer, device_id_type=pl.DeviceIdType.MESH,
         )
         copy.start()
+        started.append(copy)
         return copy
 
-    x_own = x_ref[...].reshape(cells, C).astype(jnp.float32)
+    loads[0].wait()
+    x_own = xg[j].reshape(cells, C).astype(jnp.float32)
     mean_own = jnp.sum(x_own, axis=0, keepdims=True) * (1.0 / cells)
     centered_own = x_own - mean_own
     m2_own = jnp.sum(centered_own * centered_own, axis=0, keepdims=True)
     st1[s] = jnp.concatenate([mean_own, m2_own], axis=0)
-    xg[j] = x_ref[...]
-    cg[pl.ds(F * j, F), pl.ds(1, R)] = c_ref[...]
+    for load in loads[1:4]:
+        load.wait()
 
     pl.semaphore_wait(barrier, len(peers))
 
-    started = []
     s1 = [remote(st1.at[s], st1.at[s], (j, wrap_s(s + d))) for d in range(1, S)]
     cots = []
     for d in range(1, T):
-        cots.append(remote(c_ref, cg.at[pl.ds(F * j, F), pl.ds(1, R)], (wrap_j(j + d), s)))
+        cots.append(remote(c_own_ref, c_own_ref, (wrap_j(j + d), s)))
     for d in range(T):
         cots.append(remote(
-            c_ref.at[:, pl.ds(R - 1, 1)], cg.at[pl.ds(F * j, F), pl.ds(0, 1)],
+            cg.at[pl.ds(F * j, F), pl.ds(R, 1)], cg.at[pl.ds(F * j, F), pl.ds(0, 1)],
             (wrap_j(j + d), wrap_s(s + 1))))
         cots.append(remote(
-            c_ref.at[:, pl.ds(0, 1)], cg.at[pl.ds(F * j, F), pl.ds(R + 1, 1)],
+            cg.at[pl.ds(F * j, F), pl.ds(1, 1)], cg.at[pl.ds(F * j, F), pl.ds(R + 1, 1)],
             (wrap_j(j + d), wrap_s(s - 1))))
-    xs = [remote(x_ref, xg.at[j], (wrap_j(j + d), s)) for d in range(1, T)]
-    started += s1 + cots + xs
+    xs = [remote(x_own_ref, x_own_ref, (wrap_j(j + d), s)) for d in range(1, T)]
 
     def merge(slots, n, count):
         mean = slots[0][0:1]
@@ -94,7 +103,6 @@
     mean1, m21 = merge(st1, S, float(cells))
     st2[j] = jnp.concatenate([mean1, m21], axis=0)
     s2 = [remote(st2.at[j], st2.at[j], (wrap_j(j + d), s)) for d in range(1, T)]
-    started += s2
 
     for copy in cots:
         copy.wait_recv()
@@ -112,7 +120,7 @@
         g3[pl.ds(0, TF), :, :, c * O:(c + 1) * O] = piece.astype(jnp.bfloat16).reshape(TF, R + 2, W, O)
     g3[pl.ds(TF, 2)] = jnp.zeros((2, R + 2, W, 3 * O), jnp.bfloat16)
 
-    w_copy.wait()
+    loads[4].wait()
     total = jnp.zeros((cells, C), jnp.float32)
     for a in range(3):
         for b in range(3):
@@ -159,6 +167,28 @@
     rows = lambda target: pl.ds(pl.multiple_of(target * shard + start, 32), chunk)
     hidden_t = ht[...]
     pair = []
+
+    def across(k):
+        return pltpu.make_async_remote_copy(
+            src_ref=sbuf.at[k], dst_ref=rbuf.at[z], send_sem=zs_sem.at[k], recv_sem=zr_sem.at[z],
+            device_id=(j, 2 * k + core), device_id_type=pl.DeviceIdType.MESH,
+        )
+
+    def arriving(k):
+        return pltpu.make_async_remote_copy(
+            src_ref=sbuf.at[k], dst_ref=rbuf.at[k], send_sem=zs_sem.at[k], recv_sem=zr_sem.at[k],
+            device_id=(j, 2 * k + core), device_id_type=pl.DeviceIdType.MESH,
+        )
+
+    def forward(k):
+        pair[k].wait_recv()
+
+        @pl.when(k != z)
+        def _():
+            sbuf[k] = (wg[rows(2 * k + core)] + pbuf[k]).astype(sbuf.dtype)
+            across(k).start()
+
+    sent = 0
     for a in range(3):
         for b in range(3):
             g = a * 3 + b
@@ -171,7 +201,9 @@
                 k = len(pair)
                 pair.append(remote(
                     wg.at[rows(2 * k + 1 - core)], pbuf.at[k], (j, 2 * z + 1 - core)))
-    started += pair
+                if k:
+                    forward(sent)
+                    sent += 1
 
     normed = (x_own - mean) * inv
     act = normed * gain + shift
@@ -181,17 +213,11 @@
         [jnp.sum(act_grad * normed, axis=0, keepdims=True),
          jnp.sum(act_grad, axis=0, keepdims=True)], axis=0)
     g1 = [remote(gr1.at[s], gr1.at[s], (j, wrap_s(s + d))) for d in range(1, S)]
-    started += g1
     hg[...] = act_grad
 
-    for copy in pair:
-        copy.wait_recv()
-    zs = []
-    for d in range(1, Z):
-        k = lax.rem(z + d, Z)
-        sbuf[d - 1] = (wg[rows(2 * k + core)] + pbuf[k]).astype(sbuf.dtype)
-        zs.append(remote(sbuf.at[d - 1], rbuf.at[d - 1], (j, 2 * k + core)))
-    started += zs
+    for k in range(sent, Z):
+        forward(k)
+    rbuf[z] = jnp.zeros(rbuf.shape[1:], rbuf.dtype)
 
     for copy in g1:
         copy.wait_recv()
@@ -200,15 +226,15 @@
         part = part + gr1[k]
     gr2[j] = part
     g2 = [remote(gr2.at[j], gr2.at[j], (wrap_j(j + d), s)) for d in range(1, T)]
-    started += g2
 
     acc = wg[rows(s)] + pbuf[z]
-    for d in range(1, Z):
-        zs[d - 1].wait_recv()
-        acc = acc + rbuf[d - 1].astype(jnp.float32)
+    for k in range(Z):
+        @pl.when(k != z)
+        def _():
+            arriving(k).wait_recv()
+        acc = acc + rbuf[k].astype(jnp.float32)
     abuf[j] = acc.astype(abuf.dtype)
     ag = [remote(abuf.at[j], abuf.at[j], (wrap_j(j + d), s)) for d in range(1, T)]
-    started += ag
 
     for copy in g2:
         copy.wait_recv()
@@ -232,6 +258,21 @@
         wg_out[at:at + chunk] = abuf[k].astype(jnp.float32)
     for copy in started:
         copy.wait_send()
+    for k in range(Z):
+        @pl.when(k != z)
+        def _():
+            across(k).wait_send()
+
+
+def store_kernel(*refs):
+    count = (len(refs) - 1) // 2
+    copies = [
+        pltpu.make_async_copy(refs[k], refs[count + k], refs[-1].at[k]) for k in range(count)
+    ]
+    for copy in copies:
+        copy.start()
+    for copy in copies:
+        copy.wait()
 
 
 def fused_shards(T, S, latent_clip, cotangent, conv_weight, norm_gain, norm_shift):
@@ -241,10 +282,11 @@
     chunk = -(-shard // (T * UNIT)) * UNIT
     cells = F * R * W
     Z = S // 2
-    copies = 2 * ((S - 1) + (T - 1)) + 2 * (T - 1) + 2 * T + Z + (Z - 1) + (T - 1)
+    copies = 2 * ((S - 1) + (T - 1)) + 2 * (T - 1) + 2 * T + Z + (T - 1)
     vmem = pl.BlockSpec(memory_space=pltpu.VMEM)
     f32, bf16 = jnp.float32, jnp.bfloat16
-    clip, wgrad, gg, sg = pl.pallas_call(
+    hbm = pl.BlockSpec(memory_space=pl.ANY)
+    results = pl.pallas_call(
         functools.partial(fused_kernel, T, S, shard, chunk),
         out_shape=(
             jax.ShapeDtypeStruct(latent_clip.shape, bf16),
@@ -252,9 +294,11 @@
             jax.ShapeDtypeStruct((1, C), f32),
             jax.ShapeDtypeStruct((1, C), f32),
         ),
-        in_specs=[vmem, vmem, pl.BlockSpec(memory_space=pl.ANY), vmem, vmem],
+        in_specs=[hbm] * 5,
         out_specs=(vmem, vmem, vmem, vmem),
         scratch_shapes=[
+            pltpu.VMEM((1, C), f32),
+            pltpu.VMEM((1, C), f32),
             pltpu.VMEM(conv_weight.shape, bf16),
             pltpu.VMEM((T, F, R, W, C), bf16),
             pltpu.VMEM((T * F, R + 2, W, O), bf16),
@@ -267,16 +311,25 @@
             pltpu.VMEM((C, T * cells), bf16),
             pltpu.VMEM(conv_weight.shape, f32),
             pltpu.VMEM((Z, chunk, O), f32),
-            pltpu.VMEM((Z - 1, chunk, O), bf16),
-            pltpu.VMEM((Z - 1, chunk, O), bf16),
+            pltpu.VMEM((Z, chunk, O), bf16),
+            pltpu.VMEM((Z, chunk, O), bf16),
             pltpu.VMEM((T, chunk, O), bf16),
             pltpu.SemaphoreType.DMA((copies,)),
             pltpu.SemaphoreType.DMA((copies,)),
-            pltpu.SemaphoreType.DMA,
+            pltpu.SemaphoreType.DMA((Z,)),
+            pltpu.SemaphoreType.DMA((Z,)),
+            pltpu.SemaphoreType.DMA((5,)),
         ],
         compiler_params=pltpu.CompilerParams(
-            collective_id=0, has_side_effects=True, vmem_limit_bytes=40 * 1024 * 1024),
+            collective_id=0, has_side_effects=True, vmem_limit_bytes=63 * 1024 * 1024),
     )(latent_clip, cotangent, conv_weight, norm_gain.reshape(1, C), norm_shift.reshape(1, C))
+    clip, wgrad, gg, sg = pl.pallas_call(
+        store_kernel,
+        out_shape=tuple(jax.ShapeDtypeStruct(r.shape, r.dtype) for r in results),
+        in_specs=[pl.BlockSpec(memory_space=pl.ANY)] * 4,
+        out_specs=(pl.BlockSpec(memory_space=pltpu.HBM),) * 4,
+        scratch_shapes=[pltpu.SemaphoreType.DMA((4,))],
+    )(*results)
     return clip, wgrad, gg.reshape(C), sg.reshape(C)
 
 

time: 36.9 us -> 47.4 us (1.28)
  Pallas kernels: 29 us -> 46.6 us
  local copies, waits for them, and re-layouts: 6.94 us -> 0 us
    pallas_call x0 -> x1, Pallas kernels: none -> 16.6 us  [fused_shards(): pl.pallas_call(store_kernel, out_shape=tuple((jax.ShapeDtypeStruct(r.shap...]
    unnamed x14 -> x0, local copies, waits for them, and re-layouts: 6.94 us -> none
    pallas_call x1, Pallas kernels: 29 us -> 30 us  [fused_shards(): pl.pallas_call(functools.partial(fused_kernel, T, S, shard, chunk), out_s...]
where the time goes in v2:
time: 47.4 us; the launch traced here: 47.3 us
  Pallas kernels  46.6 us (98%)
  between operations  0.64 us (1%)
    pallas_call x1, Pallas kernels, fused_shards(): pl.pallas_call(functools.partial(fused_kernel, T, S, shard, chunk), out_s...  30 us
    pallas_call x1, Pallas kernels, fused_shards(): pl.pallas_call(store_kernel, out_shape=tuple((jax.ShapeDtypeStruct(r.shap...  16.6 us

profile of v2, /device:TPU:0, one launch (start us, length us, event | category | flops | bytes accessed | tf_op | source)
XLA Modules:
  0.0 47.3 jit_solution(2822517743961366270)
XLA Ops:
  0.6 30.0 %shard_map.84 = (bf16[2,2,32,256]{3,2,1,0:T(8,128)(2,1)}, f32[864,128]{1,0:T(8,128)}, f32[1,256]{1,0:T(1,128)}, f32[1,256]{1,0:T(1,128)}) custom-call(bf16[2,2,32,256]{3,2,1,0:T(8,128)(2,1)} %x_hbm.1, bf16[2,2,32,128]{3,2,1,0:T(8,128)(2,1)} %c_hbm.1, bf16[6912,128]{1,0:T(8,128)(2,1)} %w_hbm.1, f32[1,256]{1,0:T(1,128)} %bitcast.4, f32[1,256]{1,0:T(1,128)} %bitcast.5), custom_call_target="tpu_custom_call" | custom-call | tf_op jit(solution)/shard_map/pallas_call | solution.py:289
  30.7 16.6 %shard_map.85 = (bf16[2,2,32,256]{3,2,1,0:T(8,128)(2,1)}, f32[864,128]{1,0:T(8,128)}, f32[1,256]{1,0:T(1,128)}, f32[1,256]{1,0:T(1,128)}) custom-call(bf16[2,2,32,256]{3,2,1,0:T(8,128)(2,1)} %get-tuple-element.12.refs_0_, f32[864,128]{1,0:T(8,128)} %get-tuple-element.13.refs_1_, f32[1,256]{1,0:T(1,128)} %get-tuple-element.14.refs_2_, ...), custom_call_target="tpu_custom_call" | custom-call | tf_op jit(solution)/shard_map/pallas_call | solution.py:326

commit v3 on v2

--- a/solution.py
+++ b/solution.py
@@ -14,9 +14,9 @@
 def fused_kernel(
     T, S, shard, chunk,
     x_hbm, c_hbm, w_hbm, gain_hbm, shift_hbm,
-    clip_ref, wg_out, gg_ref, sg_ref,
-    gain_ref, shift_ref, w_ref, xg, cg, g3, st1, st2, gr1, gr2, hg, ht, wg, pbuf, sbuf, rbuf, abuf,
-    send_sem, recv_sem, zs_sem, zr_sem, load_sem,
+    clip_out, parts_out, sums_out,
+    gain_ref, shift_ref, w_ref, xg, cg, g3, st1, st2, gr1, gr2, hg, ht, wg, pbuf, sbuf, rbuf, abuf, clip_ref, sums_ref,
+    send_sem, recv_sem, zs_sem, zr_sem, load_sem, store_sem,
 ):
     F, R, W, C = x_hbm.shape
     O = c_hbm.shape[-1]
@@ -75,6 +75,7 @@
     pl.semaphore_wait(barrier, len(peers))
 
     s1 = [remote(st1.at[s], st1.at[s], (j, wrap_s(s + d))) for d in range(1, S)]
+    xs = [remote(x_own_ref, x_own_ref, (wrap_j(j + d), s)) for d in range(1, T)]
     cots = []
     for d in range(1, T):
         cots.append(remote(c_own_ref, c_own_ref, (wrap_j(j + d), s)))
@@ -85,7 +86,6 @@
         cots.append(remote(
             cg.at[pl.ds(F * j, F), pl.ds(1, 1)], cg.at[pl.ds(F * j, F), pl.ds(R + 1, 1)],
             (wrap_j(j + d), wrap_s(s - 1))))
-    xs = [remote(x_own_ref, x_own_ref, (wrap_j(j + d), s)) for d in range(1, T)]
 
     def merge(slots, n, count):
         mean = slots[0][0:1]
@@ -243,36 +243,40 @@
         sums = sums + gr2[k]
     gain_grad = sums[0:1]
     shift_grad = sums[1:2]
-    gg_ref[...] = gain_grad
-    sg_ref[...] = shift_grad
+    sums_ref[...] = sums
     first = group_sum(gain * shift_grad)
     second = group_sum(gain * gain_grad)
     normed = (x_own - mean) * inv
     clip = inv * (hg[...] * gain - first * (1.0 / count) - normed * (second * (1.0 / count)))
     clip_ref[...] = clip.astype(clip_ref.dtype).reshape(clip_ref.shape)
+    stores = [
+        pltpu.make_async_copy(source, target, store_sem.at[k])
+        for k, (source, target) in enumerate((
+            (clip_ref, clip_out), (sums_ref, sums_out), (abuf, parts_out)))
+    ]
+    stores[0].start()
+    stores[1].start()
 
     for copy in ag:
         copy.wait_recv()
-    for k in range(T):
-        at = min(chunk * k, shard - chunk)
-        wg_out[at:at + chunk] = abuf[k].astype(jnp.float32)
+    stores[2].start()
     for copy in started:
         copy.wait_send()
     for k in range(Z):
         @pl.when(k != z)
         def _():
             across(k).wait_send()
-
-
-def store_kernel(*refs):
-    count = (len(refs) - 1) // 2
-    copies = [
-        pltpu.make_async_copy(refs[k], refs[count + k], refs[-1].at[k]) for k in range(count)
-    ]
-    for copy in copies:
-        copy.start()
-    for copy in copies:
-        copy.wait()
+    for store in stores:
+        store.wait()
+
+
+def store_kernel(shard, chunk, clip_in, parts_in, sums_in, clip_ref, wg_ref, gg_ref, sg_ref):
+    clip_ref[...] = clip_in[...]
+    for k in range(parts_in.shape[0]):
+        at = min(chunk * k, shard - chunk)
+        wg_ref[at:at + chunk] = parts_in[k].astype(jnp.float32)
+    gg_ref[...] = sums_in[0:1]
+    sg_ref[...] = sums_in[1:2]
 
 
 def fused_shards(T, S, latent_clip, cotangent, conv_weight, norm_gain, norm_shift):
@@ -290,12 +294,11 @@
         functools.partial(fused_kernel, T, S, shard, chunk),
         out_shape=(
             jax.ShapeDtypeStruct(latent_clip.shape, bf16),
-            jax.ShapeDtypeStruct((shard, O), f32),
-            jax.ShapeDtypeStruct((1, C), f32),
-            jax.ShapeDtypeStruct((1, C), f32),
+            jax.ShapeDtypeStruct((T, chunk, O), bf16),
+            jax.ShapeDtypeStruct((2, C), f32),
         ),
         in_specs=[hbm] * 5,
-        out_specs=(vmem, vmem, vmem, vmem),
+        out_specs=(hbm,) * 3,
         scratch_shapes=[
             pltpu.VMEM((1, C), f32),
             pltpu.VMEM((1, C), f32),
@@ -314,21 +317,28 @@
             pltpu.VMEM((Z, chunk, O), bf16),
             pltpu.VMEM((Z, chunk, O), bf16),
             pltpu.VMEM((T, chunk, O), bf16),
+            pltpu.VMEM(latent_clip.shape, bf16),
+            pltpu.VMEM((2, C), f32),
             pltpu.SemaphoreType.DMA((copies,)),
             pltpu.SemaphoreType.DMA((copies,)),
             pltpu.SemaphoreType.DMA((Z,)),
             pltpu.SemaphoreType.DMA((Z,)),
             pltpu.SemaphoreType.DMA((5,)),
+            pltpu.SemaphoreType.DMA((3,)),
         ],
         compiler_params=pltpu.CompilerParams(
             collective_id=0, has_side_effects=True, vmem_limit_bytes=63 * 1024 * 1024),
     )(latent_clip, cotangent, conv_weight, norm_gain.reshape(1, C), norm_shift.reshape(1, C))
     clip, wgrad, gg, sg = pl.pallas_call(
-        store_kernel,
-        out_shape=tuple(jax.ShapeDtypeStruct(r.shape, r.dtype) for r in results),
-        in_specs=[pl.BlockSpec(memory_space=pl.ANY)] * 4,
-        out_specs=(pl.BlockSpec(memory_space=pltpu.HBM),) * 4,
-        scratch_shapes=[pltpu.SemaphoreType.DMA((4,))],
+        functools.partial(store_kernel, shard, chunk),
+        out_shape=(
+            jax.ShapeDtypeStruct(latent_clip.shape, bf16),
+            jax.ShapeDtypeStruct((shard, O), f32),
+            jax.ShapeDtypeStruct((1, C), f32),
+            jax.ShapeDtypeStruct((1, C), f32),
+        ),
+        in_specs=[vmem] * 3,
+        out_specs=(pl.BlockSpec(memory_space=pltpu.VMEM),) * 4,
     )(*results)
     return clip, wgrad, gg.reshape(C), sg.reshape(C)
 

time: 47.4 us -> 33.8 us (0.71)
  Pallas kernels: 46.6 us -> 33 us
    pallas_call x1, Pallas kernels: 16.6 us -> 1.77 us  [fused_shards(): pl.pallas_call(functools.partial(store_kernel, shard, chunk), out_shape=(...]
    pallas_call x1, Pallas kernels: 30 us -> 31.2 us  [fused_shards(): pl.pallas_call(functools.partial(fused_kernel, T, S, shard, chunk), out_s...]
where the time goes in v3:
time: 33.8 us; the launch traced here: 33.6 us
  Pallas kernels  33 us (98%)
  between operations  0.64 us (2%)
    pallas_call x1, Pallas kernels, fused_shards(): pl.pallas_call(functools.partial(fused_kernel, T, S, shard, chunk), out_s...  31.2 us
    pallas_call x1, Pallas kernels, fused_shards(): pl.pallas_call(functools.partial(store_kernel, shard, chunk), out_shape=(...  1.77 us

profile of v3, /device:TPU:0, one launch (start us, length us, event | category | flops | bytes accessed | tf_op | source)
XLA Modules:
  0.0 33.6 jit_solution(9641821354157169348)
XLA Ops:
  0.6 31.2 %shard_map.84 = (bf16[2,2,32,256]{3,2,1,0:T(8,128)(2,1)}, bf16[4,224,128]{2,1,0:T(8,128)(2,1)}, f32[2,256]{1,0:T(2,128)}) custom-call(bf16[2,2,32,256]{3,2,1,0:T(8,128)(2,1)} %x_hbm.1, bf16[2,2,32,128]{3,2,1,0:T(8,128)(2,1)} %c_hbm.1, bf16[6912,128]{1,0:T(8,128)(2,1)} %w_hbm.1, f32[1,256]{1,0:T(1,128)} %bitcast.4, f32[1,256]{1,0:T(1,128)} %bitcast.5), custom_call_target="tpu_custom_call" | custom-call | tf_op jit(solution)/shard_map/pallas_call | solution.py:293
  31.8 1.8 %shard_map.85 = (bf16[2,2,32,256]{3,2,1,0:T(8,128)(2,1)}, f32[864,128]{1,0:T(8,128)}, f32[1,256]{1,0:T(1,128)}, f32[1,256]{1,0:T(1,128)}) custom-call(bf16[2,2,32,256]{3,2,1,0:T(8,128)(2,1)} %get-tuple-element.11.clip_in, bf16[4,224,128]{2,1,0:T(8,128)(2,1)} %get-tuple-element.12.parts_in, f32[2,256]{1,0:T(2,128)} %get-tuple-element.13.sums_in), custom_call_target="tpu_custom_call" | custom-call | tf_op jit(solution)/shard_map/pallas_call | solution.py:332

commit v4 on v3

--- a/solution.py
+++ b/solution.py
@@ -155,6 +155,16 @@
     gain = gain_ref[...]
     shift = shift_ref[...]
 
+    normed = (x_own - mean) * inv
+    act = normed * gain + shift
+    sigma = jax.nn.sigmoid(act)
+    act_grad = hg[...] * (sigma * (1.0 + act * (1.0 - sigma)))
+    gr1[s] = jnp.concatenate(
+        [jnp.sum(act_grad * normed, axis=0, keepdims=True),
+         jnp.sum(act_grad, axis=0, keepdims=True)], axis=0)
+    g1 = [remote(gr1.at[s], gr1.at[s], (j, wrap_s(s + d))) for d in range(1, S)]
+    hg[...] = act_grad
+
     for copy in xs:
         copy.wait_recv()
     for k in range(T):
@@ -197,6 +207,14 @@
             for c in range(3):
                 tap = g * 3 + c
                 wg[tap * C:(tap + 1) * C] = out[:, c * O:(c + 1) * O]
+            if g == 4:
+                for copy in g1:
+                    copy.wait_recv()
+                part = gr1[0]
+                for k in range(1, S):
+                    part = part + gr1[k]
+                gr2[j] = part
+                g2 = [remote(gr2.at[j], gr2.at[j], (wrap_j(j + d), s)) for d in range(1, T)]
             while len(pair) < Z and shard * 2 * (len(pair) + 1) <= 3 * C * (g + 1):
                 k = len(pair)
                 pair.append(remote(
@@ -205,36 +223,9 @@
                     forward(sent)
                     sent += 1
 
-    normed = (x_own - mean) * inv
-    act = normed * gain + shift
-    sigma = jax.nn.sigmoid(act)
-    act_grad = hg[...] * (sigma * (1.0 + act * (1.0 - sigma)))
-    gr1[s] = jnp.concatenate(
-        [jnp.sum(act_grad * normed, axis=0, keepdims=True),
-         jnp.sum(act_grad, axis=0, keepdims=True)], axis=0)
-    g1 = [remote(gr1.at[s], gr1.at[s], (j, wrap_s(s + d))) for d in range(1, S)]
-    hg[...] = act_grad
-
     for k in range(sent, Z):
         forward(k)
     rbuf[z] = jnp.zeros(rbuf.shape[1:], rbuf.dtype)
-
-    for copy in g1:
-        copy.wait_recv()
-    part = gr1[0]
-    for k in range(1, S):
-        part = part + gr1[k]
-    gr2[j] = part
-    g2 = [remote(gr2.at[j], gr2.at[j], (wrap_j(j + d), s)) for d in range(1, T)]
-
-    acc = wg[rows(s)] + pbuf[z]
-    for k in range(Z):
-        @pl.when(k != z)
-        def _():
-            arriving(k).wait_recv()
-        acc = acc + rbuf[k].astype(jnp.float32)
-    abuf[j] = acc.astype(abuf.dtype)
-    ag = [remote(abuf.at[j], abuf.at[j], (wrap_j(j + d), s)) for d in range(1, T)]
 
     for copy in g2:
         copy.wait_recv()
@@ -257,15 +248,28 @@
     stores[0].start()
     stores[1].start()
 
-    for copy in ag:
-        copy.wait_recv()
-    stores[2].start()
     for copy in started:
         copy.wait_send()
+
+    acc = wg[rows(s)] + pbuf[z]
+    for k in range(Z):
+        @pl.when(k != z)
+        def _():
+            arriving(k).wait_recv()
+        acc = acc + rbuf[k].astype(jnp.float32)
+    abuf[j] = acc.astype(abuf.dtype)
+    ag = [remote(abuf.at[j], abuf.at[j], (wrap_j(j + d), s)) for d in range(1, T)]
+
     for k in range(Z):
         @pl.when(k != z)
         def _():
             across(k).wait_send()
+
+    for copy in ag:
+        copy.wait_recv()
+    stores[2].start()
+    for copy in ag:
+        copy.wait_send()
     for store in stores:
         store.wait()
 

time: 33.8 us -> 32.8 us (0.970)
  Pallas kernels: 33 us -> 32 us
    pallas_call x1, Pallas kernels: 31.2 us -> 30.3 us  [fused_shards(): pl.pallas_call(functools.partial(fused_kernel, T, S, shard, chunk), out_s...]
where the time goes in v4:
time: 32.8 us; the launch traced here: 32.7 us
  Pallas kernels  32 us (98%)
  between operations  0.64 us (2%)
    pallas_call x1, Pallas kernels, fused_shards(): pl.pallas_call(functools.partial(fused_kernel, T, S, shard, chunk), out_s...  30.3 us
    pallas_call x1, Pallas kernels, fused_shards(): pl.pallas_call(functools.partial(store_kernel, shard, chunk), out_shape=(...  1.77 us

profile of v4, /device:TPU:0, one launch (start us, length us, event | category | flops | bytes accessed | tf_op | source)
XLA Modules:
  0.0 32.7 jit_solution(220013283416750251)
XLA Ops:
  0.6 30.3 %shard_map.84 = (bf16[2,2,32,256]{3,2,1,0:T(8,128)(2,1)}, bf16[4,224,128]{2,1,0:T(8,128)(2,1)}, f32[2,256]{1,0:T(2,128)}) custom-call(bf16[2,2,32,256]{3,2,1,0:T(8,128)(2,1)} %x_hbm.1, bf16[2,2,32,128]{3,2,1,0:T(8,128)(2,1)} %c_hbm.1, bf16[6912,128]{1,0:T(8,128)(2,1)} %w_hbm.1, f32[1,256]{1,0:T(1,128)} %bitcast.4, f32[1,256]{1,0:T(1,128)} %bitcast.5), custom_call_target="tpu_custom_call" | custom-call | tf_op jit(solution)/shard_map/pallas_call | solution.py:297
  30.9 1.8 %shard_map.85 = (bf16[2,2,32,256]{3,2,1,0:T(8,128)(2,1)}, f32[864,128]{1,0:T(8,128)}, f32[1,256]{1,0:T(1,128)}, f32[1,256]{1,0:T(1,128)}) custom-call(bf16[2,2,32,256]{3,2,1,0:T(8,128)(2,1)} %get-tuple-element.11.clip_in, bf16[4,224,128]{2,1,0:T(8,128)(2,1)} %get-tuple-element.12.parts_in, f32[2,256]{1,0:T(2,128)} %get-tuple-element.13.sums_in), custom_call_target="tpu_custom_call" | custom-call | tf_op jit(solution)/shard_map/pallas_call | solution.py:336
